TPU v7x, 32 devices: a whole 2x2x4 slice. The times are simulated.
32 devices in a mesh: dp: 8 (over y, x, core), mp: 4 (over z).
Axes of the slice: x: 2, y: 2, z: 4, core: 2. Of those that a mesh axis runs over, the one named last changes fastest.
Arguments:
- gradients: bfloat16 [8, 2, 8192, 1024], P('dp', None, None, 'mp'), may hold values from -16 to 16
- feedback: bfloat16 [8, 2, 8192, 1024], P('dp', None, None, 'mp'), may hold values from -1.796875 to 1.796875
- right_factor: float32 [2, 1024, 16], P(None, 'mp'), may hold values from -6 to 6
Outputs:
- new_feedback: bfloat16 [8, 2, 8192, 1024], P('dp', None, None, 'mp')
- update: bfloat16 [2, 8192, 1024], P(None, 'dp', 'mp')
All inputs are finite; a program needn't handle non-finite values.
Results may differ from a plain program's by a relative error of at most 0.0095.
Values may be sent and summed in bfloat16 or wider, within the bound.
A program may use at most 64 MiB of HBM per device.

v0:
```python
import jax
import jax.numpy as jnp
from jax import lax
from jax.sharding import PartitionSpec as P


def gram_columns(factor_rows, gram_matrix):
    lower_factor = jnp.linalg.cholesky(gram_matrix)
    return lax.linalg.triangular_solve(
        lower_factor, factor_rows, left_side=False, lower=True, transpose_a=True
    )


def shards(gradients, feedback, right_factor):
    replicas = lax.axis_size("dp")
    row_count = gradients.shape[2] // replicas
    compensated = (gradients.astype(jnp.float32) + feedback.astype(jnp.float32)).astype(
        jnp.bfloat16
    )
    right_start = right_factor.astype(jnp.bfloat16)
    partial_value = (
        jnp.einsum("imdc,mcr->mdr", compensated, right_start, preferred_element_type=jnp.float32)
        / replicas
    )
    left_total = lax.psum(partial_value, ("dp", "mp"))
    gram_matrix = jnp.einsum(
        "mdr,mds->mrs", left_total, left_total, precision=lax.Precision.HIGHEST
    )
    left_orth = gram_columns(left_total, gram_matrix)
    left_low = left_orth.astype(jnp.bfloat16)
    right_part = (
        jnp.einsum("imdc,mdr->mcr", compensated, left_low, preferred_element_type=jnp.float32)
        / replicas
    )
    right_total = lax.psum(right_part, "dp")
    right_low = right_total.astype(jnp.bfloat16)
    approx = jnp.einsum("mdr,mcr->mdc", left_low, right_low, preferred_element_type=jnp.float32)
    new_feedback = (compensated.astype(jnp.float32) - approx[None]).astype(jnp.bfloat16)
    update = lax.dynamic_slice_in_dim(
        approx, lax.axis_index("dp") * row_count, row_count, 1
    ).astype(jnp.bfloat16)
    return (new_feedback, update)


def solution(mesh):
    return jax.shard_map(
        shards,
        mesh=mesh,
        in_specs=(P("dp", None, None, "mp"), P("dp", None, None, "mp"), P(None, "mp", None)),
        out_specs=(P("dp", None, None, "mp"), P(None, "dp", "mp")),
        check_vma=False,
    )
```

profile of v0, /device:TPU:0, one launch (start us, length us, event | category | flops | bytes accessed | tf_op | source)
XLA Modules:
  0.0 210.4 jit_solution(9249513478611784968)
XLA Ops:
  7.2 0.0 all-reduce.2.cloned.1.call-start
  7.2 9.0 %convolution_multiply_fusion = f32[2,8192,16]{1,2,0:T(8,128)} fusion(f32[2,256,16]{1,2,0:T(8,128)} %param.5, bf16[1,2,8192,256]{3,2,1,0:T(8,128)(2,1)} %param.4, bf16[1,2,8192,256]{3,2,1,0:T(8,128)(2,1)} %param.3), kind=kOutput, calls=%fused_computation.3 | convolution fusion | flops 151265280 | bytes 17858560 | tf_op jit(solution)/shard_map/imdc,mcr->mdr/dot_general | solution.py:22
  16.3 0.0 all-reduce.2.cloned.1.call-update
  16.3 132.7 %all-reduce.2.cloned.1.call-done = f32[2,8192,16]{1,2,0:T(8,128)} async-done(((f32[2,8192,16]{1,2,0:T(8,128)}), f32[2,8192,16]{1,2,0:T(8,128)}) %all-reduce.2.cloned.1.call-update) | async-done | bytes 1048592 | tf_op jit(solution)/shard_map/psum | solution.py:25
  149.0 3.0 %fusion.12 = f32[2,16,16]{2,1,0:T(8,128)S(1)} fusion(f32[2,8192,16]{1,2,0:T(8,128)} %all-reduce.2.cloned.1.call-done), kind=kOutput, calls=%fused_computation.21 | convolution fusion | flops 50331648 | bytes 1050624 | tf_op jit(solution)/shard_map/mdr,mds->mrs/dot_general | solution.py:26
  152.1 0.1 copy.7
  152.1 2.9 %custom-call.7 = f32[2,16,16]{2,1,0:T(8,128)S(1)} custom-call(f32[2,16,16]{2,1,0:T(8,128)S(1)} %fusion.8), custom_call_target="Cholesky" | custom-call | tf_op jit(solution)/shard_map/jit(cholesky)/cholesky | solution.py:8
  155.1 0.1 compare_reduce_fusion
  155.2 0.1 select_bitcast_fusion
  155.3 2.5 %custom-call.8 = f32[2,1,16,16]{2,3,1,0:T(8,128)S(1)} custom-call(f32[2,1,16,16]{3,2,1,0:T(8,128)S(1)} %select_bitcast_fusion), custom_call_target="InvertDiagBlocksLowerTriangular" | custom-call | tf_op jit(solution)/shard_map/triangular_solve | solution.py:9
  157.8 2.3 %convolution_convert_fusion = bf16[2,8192,16]{1,2,0:T(8,128)(2,1)S(1)} fusion(f32[2,8192,16]{1,2,0:T(8,128)} %all-reduce.2.cloned.1.call-done, f32[2,1,16,16]{2,3,1,0:T(8,128)S(1)} %custom-call.8), kind=kOutput, calls=%fused_computation.4 | convolution fusion | flops 50593792 | bytes 1574912 | tf_op jit(solution)/shard_map/triangular_solve | solution.py:9
  160.0 7.8 %fusion.4 = f32[2,256,16]{1,2,0:T(8,128)S(1)} fusion(bf16[2,8192,16]{1,2,0:T(8,128)(2,1)S(1)} %convolution_convert_fusion, bf16[1,2,8192,256]{3,2,1,0:T(8,128)(2,1)} %param.4, bf16[1,2,8192,256]{3,2,1,0:T(8,128)(2,1)} %param.3), kind=kOutput, calls=%fused_computation.9 | convolution fusion | flops 151003136 | bytes 17334272 | tf_op jit(solution)/shard_map/imdc,mdr->mcr/dot_general | solution.py:32
  167.8 22.4 %psum.15 = bf16[2,256,16]{1,2,0:T(8,128)(2,1)S(1)} all-reduce(f32[2,256,16]{1,2,0:T(8,128)S(1)} %fusion.4), channel_id=1, replica_groups=mesh['dp'=8,'mp'=4] {'dp'}, use_global_device_ids=true, to_apply=%region_3.4 | all-reduce | flops 8192 | bytes 49152 | tf_op jit(solution)/shard_map/psum | solution.py:35
  190.2 11.1 %fusion = (bf16[1,2,8192,256]{3,2,1,0:T(8,128)(2,1)}, bf16[2,8192,256]{2,1,0:T(8,128)(2,1)}) fusion(bf16[1,2,8192,256]{3,2,1,0:T(8,128)(2,1)} %param.4, bf16[1,2,8192,256]{3,2,1,0:T(8,128)(2,1)} %param.3, bf16[2,8192,16]{1,2,0:T(8,128)(2,1)S(1)} %convolution_convert_fusion, bf16[2,256,16]{1,2,0:T(8,128)(2,1)S(1)} %psum.15), kind=kOutput, calls=%fused_computation.1 | convolution fusion | flops 167772160 | bytes 34095104 | tf_op jit(solution)/shard_map/mdr,mcr->mdc/dot_general | solution.py:37
  201.3 2.3 %dynamic-slice_convert_fusion = bf16[2,1024,256]{2,1,0:T(8,128)(2,1)} fusion(bf16[2,8192,256]{2,1,0:T(8,128)(2,1)} %get-tuple-element.3, s32[]{:T(128)S(6)} %select_n.8), kind=kLoop, calls=%fused_computation.8 | loop fusion | bytes 2097156 | tf_op jit(solution)/shard_map/convert_element_type | solution.py:41
  (4 shorter events, 0.1 us)
Async XLA Ops:
  7.2 141.9 %all-reduce.2.cloned.1.call-start = ((), (), s32[]{:S(2)}) async-start(), calls=%async_computation | async-start | bytes 2097152 | tf_op jit(solution)/shard_map/psum | solution.py:25
Sparse Core Ops, SparseCore 0:
  16.4 132.5 all-reduce.1
where the time goes:
time: 211 us; the launch traced here: 210 us
  waiting for transfers between devices  133 us (63%)
  matrix products  33.3 us (16%)
  blocking collectives  22.4 us (11%)
  between operations  14.1 us (7%)
  other arithmetic  5.64 us (3%)
  local copies, waits for them, and re-layouts  2.33 us (1%)
    psum x1, waiting for transfers between devices, shards(): left_total = lax.psum(partial_value, ('dp', 'mp'))  133 us
    psum x1, blocking collectives, shards(): right_total = lax.psum(right_part, 'dp')  22.4 us
    dot_general x1, matrix products, shards(): jnp.einsum('mdr,mcr->mdc', left_low, right_low, preferred_element_type=jn...  11.1 us
    dot_general x1, matrix products, shards(): jnp.einsum('imdc,mcr->mdr', compensated, right_start, preferred_element_t...  9.04 us
    dot_general x1, matrix products, shards(): jnp.einsum('imdc,mdr->mcr', compensated, left_low, preferred_element_type...  7.79 us
  transfers between devices with their start and end apart: 1, of which 1 were waited for; matrix products, arithmetic and copies ran while one was open for 0% of the time, Pallas kernels for 0%

commit v1 on v0

v1 whole, which is shorter than its diff:
```python
import functools

import jax
import jax.numpy as jnp
from jax import lax
from jax.experimental import pallas as pl
from jax.experimental.pallas import tpu as pltpu
from jax.sharding import PartitionSpec as P

LANES = 128
CORES = 2
F32 = jnp.float32
BF16 = jnp.bfloat16


def split3(value):
    high = value.astype(BF16)
    rest = value - high.astype(F32)
    middle = rest.astype(BF16)
    low = (rest - middle.astype(F32)).astype(BF16)
    return high, middle, low


def nt_dot(left, right):
    return lax.dot_general(left, right, (((1,), (1,)), ((), ())), preferred_element_type=F32)


def nn_dot(left, right):
    return lax.dot_general(left, right, (((1,), (0,)), ((), ())), preferred_element_type=F32)


def reduce_kernel(
    n_dp, n_mp,
    grad_hbm, feed_hbm, right_ref,
    comp_hbm, q_hbm, right_low_ref,
    comp, feed, part, half, from_core, from_chip, plane, from_z, full,
    gram_chip, gram_core, q_low, right_all,
    load_sem, store_sem, qstore_sem,
    core_send, core_recv, chip_send, chip_recv, z_send, z_recv,
    zg_send, zg_recv, cg_send, cg_recv, kg_send, kg_recv,
    gc_send, gc_recv, gk_send, gk_recv, r_send, r_recv,
):
    mats, rows, cols = comp.shape
    rank = right_ref.shape[2]
    blocks = rows // LANES
    tile = q_low.shape[3]
    tiles = rows // tile
    per_tile = tile // LANES
    chips = n_dp // CORES
    half_blocks = blocks // CORES
    chip_blocks = half_blocks // chips
    z_split = chip_blocks % n_mp == 0
    z_blocks = chip_blocks // n_mp if z_split else chip_blocks

    dp = lax.axis_index("dp")
    z = lax.axis_index("mp")
    core = lax.rem(dp, CORES)
    chip = dp // CORES
    other = 1 - core
    twin = chip * CORES + other

    def loads(m, t):
        span = pl.ds(t * tile, tile)
        return (
            pltpu.make_async_copy(grad_hbm.at[0, m, span], comp.at[m, span], load_sem.at[0, m, t]),
            pltpu.make_async_copy(feed_hbm.at[0, m, span], feed.at[m, span], load_sem.at[1, m, t]),
        )

    for m in range(mats):
        def start_loads(t, carry, m=m):
            for copy in loads(m, t):
                copy.start()
            return carry
        lax.fori_loop(0, tiles, start_loads, 0)

    barrier = pltpu.get_barrier_semaphore()
    for k in range(1, n_dp):
        pl.semaphore_signal(barrier, inc=1, device_id=(lax.rem(dp + k, n_dp), z),
                            device_id_type=pl.DeviceIdType.MESH)
    for k in range(1, n_mp):
        pl.semaphore_signal(barrier, inc=1, device_id=(dp, lax.rem(z + k, n_mp)),
                            device_id_type=pl.DeviceIdType.MESH)
    pl.semaphore_wait(barrier, n_dp - 1 + n_mp - 1)

    sent = []

    def remote(src, dst, send_sem, recv_sem, device):
        return pltpu.make_async_remote_copy(
            src_ref=src, dst_ref=dst, send_sem=send_sem, recv_sem=recv_sem,
            device_id=device, device_id_type=pl.DeviceIdType.MESH)

    def send(*args):
        copy = remote(*args)
        copy.start()
        sent.append(copy)

    def landed(dst, send_sem, recv_sem):
        remote(dst, dst, send_sem, recv_sem, (twin, z)).wait_recv()

    eye = (lax.broadcasted_iota(jnp.int32, (rank, rank), 0)
           == lax.broadcasted_iota(jnp.int32, (rank, rank), 1)).astype(BF16)

    def compensate(m, first, last):
        right_t = nt_dot(eye, right_ref[m].astype(BF16)).astype(BF16)

        def body(t, carry):
            for copy in loads(m, t):
                copy.wait()
            span = pl.ds(pl.multiple_of(t * tile, tile), tile)
            value = (comp[m, span].astype(F32) + feed[m, span].astype(F32)).astype(BF16)
            comp[m, span] = value
            term = nt_dot(right_t, value)
            for j in range(per_tile):
                part[m, t * per_tile + j] = term[:, j * LANES:(j + 1) * LANES]
            pltpu.make_async_copy(comp.at[m, span], comp_hbm.at[m, span], store_sem.at[m, t]).start()
            return carry
        lax.fori_loop(first, last, body, 0)

    def core_start(m):
        send(part.at[m, pl.ds(other * half_blocks, half_blocks)], from_core.at[m],
             core_send.at[m], core_recv.at[m], (twin, z))

    def core_finish(m):
        landed(from_core.at[m], core_send.at[m], core_recv.at[m])
        half[m] = part[m, pl.ds(core * half_blocks, half_blocks)] + from_core[m]

    def chip_start(m):
        for k in range(1, chips):
            to = lax.rem(chip + k, chips)
            send(half.at[m, pl.ds(to * chip_blocks, chip_blocks)], from_chip.at[m, chip],
                 chip_send.at[m, k], chip_recv.at[m, chip], (to * CORES + core, z))

    def chip_finish(m):
        total = half[m, pl.ds(chip * chip_blocks, chip_blocks)]
        for k in range(1, chips):
            source = lax.rem(chip + k, chips)
            landed(from_chip.at[m, source], chip_send.at[m, k], chip_recv.at[m, source])
            total = total + from_chip[m, source]
        plane[m] = total

    def z_start(m):
        for k in range(1, n_mp):
            to = lax.rem(z + k, n_mp)
            first = to * z_blocks if z_split else 0
            send(plane.at[m, pl.ds(first, z_blocks)], from_z.at[m, z],
                 z_send.at[m, k], z_recv.at[m, z], (dp, to))

    base = core * half_blocks + chip * chip_blocks
    mine = pl.ds(base + (z * z_blocks if z_split else 0), z_blocks)

    def z_finish(m):
        total = plane[m, pl.ds(z * z_blocks if z_split else 0, z_blocks)]
        for k in range(1, n_mp):
            source = lax.rem(z + k, n_mp)
            landed(from_z.at[m, source], z_send.at[m, k], z_recv.at[m, source])
            total = total + from_z[m, source]
        full[m, mine] = total * (1.0 / n_dp)

    def z_gather_start(m):
        if z_split:
            for k in range(1, n_mp):
                send(full.at[m, mine], full.at[m, mine], zg_send.at[m, k], zg_recv.at[m, z],
                     (dp, lax.rem(z + k, n_mp)))

    def z_gather_finish(m):
        if z_split:
            for k in range(1, n_mp):
                source = lax.rem(z + k, n_mp)
                landed(full.at[m, pl.ds(base + source * z_blocks, z_blocks)],
                       zg_send.at[m, k], zg_recv.at[m, source])

    gram_lane = 6 * rank

    def chip_gather_start(m):
        own = pl.ds(base, chip_blocks)
        for k in range(1, chips):
            to = lax.rem(chip + k, chips)
            send(full.at[m, own], full.at[m, own], cg_send.at[m, k], cg_recv.at[m, chip],
                 (to * CORES + core, z))
        value = jnp.concatenate([full[m, base + j] for j in range(chip_blocks)], axis=1)
        terms = split3(value)
        tall = jnp.concatenate(terms, axis=0)
        pad = jnp.zeros((gram_lane, value.shape[1]), BF16)
        wide = sum(nt_dot(tall, jnp.concatenate([pad, term], axis=0)) for term in terms)
        gram = wide[0:rank] + wide[rank:2 * rank] + wide[2 * rank:3 * rank]
        gram_chip[m, chip] = jnp.zeros((rank, LANES), F32)
        gram_chip[m, chip, :, 0:gram_lane + rank] = gram
        for k in range(1, chips):
            to = lax.rem(chip + k, chips)
            send(gram_chip.at[m, chip], gram_chip.at[m, chip], gc_send.at[m, k],
                 gc_recv.at[m, chip], (to * CORES + core, z))

    def chip_gather_finish(m):
        for k in range(1, chips):
            source = lax.rem(chip + k, chips)
            landed(full.at[m, pl.ds(core * half_blocks + source * chip_blocks, chip_blocks)],
                   cg_send.at[m, k], cg_recv.at[m, source])
            landed(gram_chip.at[m, source], gc_send.at[m, k], gc_recv.at[m, source])

    def core_gather_start(m):
        own = pl.ds(core * half_blocks, half_blocks)
        send(full.at[m, own], full.at[m, own], kg_send.at[m], kg_recv.at[m], (twin, z))
        total = gram_chip[m, 0]
        for c in range(1, chips):
            total = total + gram_chip[m, c]
        gram_core[m, core] = total
        send(gram_core.at[m, core], gram_core.at[m, core], gk_send.at[m], gk_recv.at[m], (twin, z))

    def core_gather_finish(m):
        landed(gram_core.at[m, other], gk_send.at[m], gk_recv.at[m])
        landed(full.at[m, pl.ds(other * half_blocks, half_blocks)], kg_send.at[m], kg_recv.at[m])

    row_at = lax.broadcasted_iota(jnp.int32, (rank, LANES), 0)
    lane_at = lax.broadcasted_iota(jnp.int32, (rank, LANES), 1)

    def inverse_factor(m):
        gram = gram_core[m, 0]
        for c in range(1, CORES):
            gram = gram + gram_core[m, c]
        copies = (lane_at < gram_lane) & (lax.rem(lane_at, rank) == row_at)
        work = jnp.where(copies, 1.0, gram)
        for k in range(rank):
            column = work[:, gram_lane + k:gram_lane + k + 1]
            row = work[k:k + 1]
            pivot = work[k:k + 1, gram_lane + k:gram_lane + k + 1]
            factor = jnp.where(row_at > k, column / pivot, 0.0)
            work = work - factor * row
        diagonal = jnp.sum(jnp.where(lane_at == row_at + gram_lane, work, 0.0), axis=1, keepdims=True)
        return work / jnp.sqrt(diagonal)

    def project(m):
        inverse = inverse_factor(m)
        high, middle, low = split3(inverse)
        group = lane_at // rank
        left = jnp.where((group == 2) | (group == 3), middle.astype(F32),
                         jnp.where(group == 5, low.astype(F32), high.astype(F32))).astype(BF16)
        left = left[:, 0:gram_lane]

        def body(t, total):
            value = jnp.concatenate([full[m, t * per_tile + j] for j in range(per_tile)], axis=1)
            xh, xm, xl = split3(value)
            q = nn_dot(left, jnp.concatenate([xh, xm, xh, xm, xl, xh], axis=0)).astype(BF16)
            q_low[m, t] = q
            span = pl.ds(pl.multiple_of(t * tile, tile), tile)
            return total + nn_dot(q, comp[m, span])
        total = lax.fori_loop(0, tiles, body, jnp.zeros((rank, cols), F32))
        right_all[m, dp] = total
        for k in range(1, n_dp):
            send(right_all.at[m, dp], right_all.at[m, dp], r_send.at[m, k], r_recv.at[m, dp],
                 (lax.rem(dp + k, n_dp), z))
        pltpu.make_async_copy(q_low.at[m], q_hbm.at[m], qstore_sem.at[m]).start()

    def right_finish(m):
        for k in range(1, n_dp):
            source = lax.rem(dp + k, n_dp)
            landed(right_all.at[m, source], r_send.at[m, k], r_recv.at[m, source])
        total = right_all[m, 0]
        for c in range(1, n_dp):
            total = total + right_all[m, c]
        right_low_ref[m] = (total * (1.0 / n_dp)).astype(BF16)

    pairs = [(core_finish, chip_start), (chip_finish, z_start), (z_finish, z_gather_start),
             (z_gather_finish, chip_gather_start), (chip_gather_finish, core_gather_start)]

    def advance(m, stage):
        for step in pairs[stage]:
            step(m)

    compensate(0, 0, tiles)
    core_start(0)
    compensate(1, 0, tiles // 2)
    advance(0, 0)
    compensate(1, tiles // 2, tiles)
    core_start(1)
    advance(0, 1)
    advance(1, 0)
    advance(0, 2)
    advance(1, 1)
    advance(0, 3)
    advance(1, 2)
    advance(0, 4)
    advance(1, 3)
    core_gather_finish(0)
    project(0)
    advance(1, 4)
    core_gather_finish(1)
    project(1)
    right_finish(0)
    right_finish(1)
    for copy in sent:
        copy.wait_send()
    for m in range(mats):
        pltpu.make_async_copy(q_low.at[m], q_hbm.at[m], qstore_sem.at[m]).wait()

        def end_store(t, carry, m=m):
            span = pl.ds(t * tile, tile)
            pltpu.make_async_copy(comp.at[m, span], comp_hbm.at[m, span], store_sem.at[m, t]).wait()
            return carry
        lax.fori_loop(0, tiles, end_store, 0)


def residue_kernel(comp_ref, q_ref, right_ref, feed_ref, update_ref):
    approx = lax.dot_general(q_ref[0, 0], right_ref[0], (((0,), (0,)), ((), ())),
                             preferred_element_type=F32)
    feed_ref[0, 0] = (comp_ref[0].astype(F32) - approx).astype(BF16)

    @pl.when(pl.program_id(1) == lax.axis_index("dp"))
    def _():
        update_ref[0] = approx.astype(BF16)


def shards(n_dp, n_mp, gradients, feedback, right_factor):
    _, mats, rows, cols = gradients.shape
    rank = right_factor.shape[2]
    tile = rows // n_dp
    tiles = rows // tile
    blocks = rows // LANES
    half_blocks = blocks // CORES
    chips = n_dp // CORES
    chip_blocks = half_blocks // chips
    z_blocks = chip_blocks // n_mp if chip_blocks % n_mp == 0 else chip_blocks
    dma = pltpu.SemaphoreType.DMA
    any_spec = pl.BlockSpec(memory_space=pl.ANY)
    vmem_spec = pl.BlockSpec(memory_space=pltpu.VMEM)
    comp, q_low, right_low = pl.pallas_call(
        functools.partial(reduce_kernel, n_dp, n_mp),
        out_shape=(
            jax.ShapeDtypeStruct((mats, rows, cols), BF16),
            jax.ShapeDtypeStruct((mats, tiles, rank, tile), BF16),
            jax.ShapeDtypeStruct((mats, rank, cols), BF16),
        ),
        in_specs=[any_spec, any_spec, vmem_spec],
        out_specs=(any_spec, any_spec, vmem_spec),
        scratch_shapes=[
            pltpu.VMEM((mats, rows, cols), BF16),
            pltpu.VMEM((mats, rows, cols), BF16),
            pltpu.VMEM((mats, blocks, rank, LANES), F32),
            pltpu.VMEM((mats, half_blocks, rank, LANES), F32),
            pltpu.VMEM((mats, half_blocks, rank, LANES), F32),
            pltpu.VMEM((mats, chips, chip_blocks, rank, LANES), F32),
            pltpu.VMEM((mats, chip_blocks, rank, LANES), F32),
            pltpu.VMEM((mats, n_mp, z_blocks, rank, LANES), F32),
            pltpu.VMEM((mats, blocks, rank, LANES), F32),
            pltpu.VMEM((mats, chips, rank, LANES), F32),
            pltpu.VMEM((mats, CORES, rank, LANES), F32),
            pltpu.VMEM((mats, tiles, rank, tile), BF16),
            pltpu.VMEM((mats, n_dp, rank, cols), F32),
            dma((2, mats, tiles)), dma((mats, tiles)), dma((mats,)),
            dma((mats,)), dma((mats,)), dma((mats, chips)), dma((mats, chips)),
            dma((mats, n_mp)), dma((mats, n_mp)),
            dma((mats, n_mp)), dma((mats, n_mp)), dma((mats, chips)), dma((mats, chips)),
            dma((mats,)), dma((mats,)),
            dma((mats, chips)), dma((mats, chips)), dma((mats,)), dma((mats,)),
            dma((mats, n_dp)), dma((mats, n_dp)),
        ],
        compiler_params=pltpu.CompilerParams(
            collective_id=0, has_side_effects=True, vmem_limit_bytes=48 * 1024 * 1024),
        name="reduce_factors",
    )(gradients, feedback, right_factor)
    return pl.pallas_call(
        residue_kernel,
        grid=(mats, tiles),
        out_shape=(
            jax.ShapeDtypeStruct((1, mats, rows, cols), BF16),
            jax.ShapeDtypeStruct((mats, tile, cols), BF16),
        ),
        in_specs=[
            pl.BlockSpec((1, tile, cols), lambda m, t: (m, t, 0)),
            pl.BlockSpec((1, 1, rank, tile), lambda m, t: (m, t, 0, 0)),
            pl.BlockSpec((1, rank, cols), lambda m, t: (m, 0, 0)),
        ],
        out_specs=(
            pl.BlockSpec((1, 1, tile, cols), lambda m, t: (0, m, t, 0)),
            pl.BlockSpec((1, tile, cols), lambda m, t: (m, 0, 0)),
        ),
        compiler_params=pltpu.CompilerParams(vmem_limit_bytes=24 * 1024 * 1024),
        name="subtract_approx",
    )(comp, q_low, right_low)


def solution(mesh):
    return jax.shard_map(
        functools.partial(shards, mesh.shape["dp"], mesh.shape["mp"]),
        mesh=mesh,
        in_specs=(P("dp", None, None, "mp"), P("dp", None, None, "mp"), P(None, "mp", None)),
        out_specs=(P("dp", None, None, "mp"), P(None, "dp", "mp")),
        check_vma=False,
    )
```

time: 211 us -> 57 us (0.27)
  waiting for transfers between devices: 133 us -> 0 us
  Pallas kernels: 0 us -> 51.8 us
  matrix products: 33.3 us -> 0 us
  blocking collectives: 22.4 us -> 0 us
  between operations: 14.1 us -> 0.65 us
  other arithmetic: 5.64 us -> 0 us
    psum x1 -> x0, waiting for transfers between devices: 133 us -> none  [shards(): left_total = lax.psum(partial_value, ('dp', 'mp'))]
    pallas_call x0 -> x2, Pallas kernels: none -> 51.8 us  [the longest x1 42.1 us: shards(): pl.pallas_call(functools.partial(reduce_kernel, n_dp, n_mp), out_shape=(j...]
    dot_general x4 -> x0, matrix products: 31 us -> none  [the longest x1 11.1 us: shards(): jnp.einsum('mdr,mcr->mdc', left_low, right_low, preferred_element_type=jn...]
    psum x1 -> x0, blocking collectives: 22.4 us -> none  [shards(): right_total = lax.psum(right_part, 'dp')]
    another operation x7 -> x0, other arithmetic: 5.63 us -> none  [the longest x4 3.09 us: gram_columns(): lower_factor = jnp.linalg.cholesky(gram_matrix)]
    unnamed x0 -> x3, local copies, waits for them, and re-layouts: none -> 4.25 us
    another operation x1 -> x0, matrix products: 2.27 us -> none  [gram_columns(): lax.linalg.triangular_solve(lower_factor, factor_rows, left_side=False, l...]
    convert_element_type x1 -> x0, local copies, waits for them, and re-layouts: 2.26 us -> none  [shards(): update = lax.dynamic_slice_in_dim(approx, lax.axis_index('dp') * row_coun...]
  transfers between devices with their start and end apart: 1 -> 0, of which waited for: 1 -> 0; matrix products, arithmetic and copies ran while one was open for 0% -> 0% of each run, Pallas kernels for 0% -> 0%
where the time goes in v1:
time: 57 us; the launch traced here: 56.8 us
  Pallas kernels  51.8 us (91%)
  local copies, waits for them, and re-layouts  4.25 us (7%)
  between operations  0.65 us (1%)
    pallas_call x1, Pallas kernels, shards(): pl.pallas_call(functools.partial(reduce_kernel, n_dp, n_mp), out_shape=(j...  42.1 us
    pallas_call x1, Pallas kernels, shards(): pl.pallas_call(residue_kernel, grid=(mats, tiles), out_shape=(jax.ShapeDt...  9.75 us
    unnamed x3, local copies, waits for them, and re-layouts  4.25 us

profile of v1, /device:TPU:0, one launch (start us, length us, event | category | flops | bytes accessed | tf_op | source)
XLA Modules:
  0.0 56.8 jit_solution(13127695465800971191)
XLA Ops:
  0.6 0.9 %copy.5.right_ref = f32[2,256,16]{2,1,0:T(8,128)S(1)} copy(f32[2,256,16]{1,2,0:T(8,128)} %param.5) | data formatting | bytes 65536 | tf_op args[2]
  1.5 42.1 %reduce_factors.1 = (bf16[2,8192,256]{2,1,0:T(8,128)(2,1)}, bf16[2,8,16,1024]{3,2,1,0:T(8,128)(2,1)S(1)}, bf16[2,16,256]{2,1,0:T(8,128)(2,1)S(1)}) custom-call(bf16[1,2,8192,256]{3,2,1,0:T(8,128)(2,1)} %grad_hbm.1, bf16[1,2,8192,256]{3,2,1,0:T(8,128)(2,1)} %feed_hbm.1, f32[2,256,16]{2,1,0:T(8,128)S(1)} %copy.5.right_ref), custom_call_target="tpu_custom_call" | custom-call | tf_op jit(solution)/shard_map/reduce_factors/pallas_call | solution.py:325
  43.6 0.0 copy-start
  43.6 3.4 %copy-done = bf16[2,8192,256]{2,1,0:T(8,128)(2,1)S(1)} copy-done((bf16[2,8192,256]{2,1,0:T(8,128)(2,1)S(1)}, bf16[2,8192,256]{2,1,0:T(8,128)(2,1)}, u32[]{:S(2)}) %copy-start) | copy-done | bytes 8388632
  47.0 9.8 %subtract_approx.1 = (bf16[1,2,8192,256]{3,2,1,0:T(8,128)(2,1)}, bf16[2,1024,256]{2,1,0:T(8,128)(2,1)}) custom-call(bf16[2,8192,256]{2,1,0:T(8,128)(2,1)S(1)} %copy-done, bf16[2,8,16,1024]{3,2,1,0:T(8,128)(2,1)S(1)} %get-tuple-element.6.q_ref, bf16[2,16,256]{2,1,0:T(8,128)(2,1)S(1)} %get-tuple-element.7.right_ref), custom_call_target="tpu_custom_call" | custom-call | tf_op jit(solution)/shard_map/subtract_approx/pallas_call | solution.py:360
Async XLA Ops:
  43.6 3.4 %copy-start = (bf16[2,8192,256]{2,1,0:T(8,128)(2,1)S(1)}, bf16[2,8192,256]{2,1,0:T(8,128)(2,1)}, u32[]{:S(2)}) copy-start(bf16[2,8192,256]{2,1,0:T(8,128)(2,1)} %get-tuple-element.5.comp_ref) | copy-start | bytes 25165828

commit v2 on v1

--- a/solution.py
+++ b/solution.py
@@ -41,7 +41,7 @@
     gc_send, gc_recv, gk_send, gk_recv, r_send, r_recv,
 ):
     mats, rows, cols = comp.shape
-    rank = right_ref.shape[2]
+    rank = right_ref.shape[1]
     blocks = rows // LANES
     tile = q_low.shape[3]
     tiles = rows // tile
@@ -97,11 +97,8 @@
     def landed(dst, send_sem, recv_sem):
         remote(dst, dst, send_sem, recv_sem, (twin, z)).wait_recv()
 
-    eye = (lax.broadcasted_iota(jnp.int32, (rank, rank), 0)
-           == lax.broadcasted_iota(jnp.int32, (rank, rank), 1)).astype(BF16)
-
     def compensate(m, first, last):
-        right_t = nt_dot(eye, right_ref[m].astype(BF16)).astype(BF16)
+        right_t = right_ref[m].astype(BF16)
 
         def body(t, carry):
             for copy in loads(m, t):
@@ -243,7 +240,7 @@
             q_low[m, t] = q
             span = pl.ds(pl.multiple_of(t * tile, tile), tile)
             return total + nn_dot(q, comp[m, span])
-        total = lax.fori_loop(0, tiles, body, jnp.zeros((rank, cols), F32))
+        total = lax.fori_loop(0, tiles, body, jnp.zeros((rank, cols), F32), unroll=4)
         right_all[m, dp] = total
         for k in range(1, n_dp):
             send(right_all.at[m, dp], right_all.at[m, dp], r_send.at[m, k], r_recv.at[m, dp],
@@ -299,14 +296,52 @@
         lax.fori_loop(0, tiles, end_store, 0)
 
 
-def residue_kernel(comp_ref, q_ref, right_ref, feed_ref, update_ref):
-    approx = lax.dot_general(q_ref[0, 0], right_ref[0], (((0,), (0,)), ((), ())),
-                             preferred_element_type=F32)
-    feed_ref[0, 0] = (comp_ref[0].astype(F32) - approx).astype(BF16)
-
-    @pl.when(pl.program_id(1) == lax.axis_index("dp"))
-    def _():
-        update_ref[0] = approx.astype(BF16)
+def residue_kernel(comp_hbm, q_hbm, right_ref, feed_hbm, update_hbm, comp, q_low, out, update,
+                   load_sem, q_sem, store_sem, update_sem):
+    mats, tiles, _, tile = q_low.shape
+    dp = lax.axis_index("dp")
+
+    def load(m, t):
+        span = pl.ds(t * tile, tile)
+        return pltpu.make_async_copy(comp_hbm.at[m, span], comp.at[m, span], load_sem.at[m, t])
+
+    def store(m, t):
+        span = pl.ds(t * tile, tile)
+        return pltpu.make_async_copy(out.at[m, span], feed_hbm.at[0, m, span], store_sem.at[m, t])
+
+    q_copies = [pltpu.make_async_copy(q_hbm.at[m], q_low.at[m], q_sem.at[m]) for m in range(mats)]
+    for m in range(mats):
+        q_copies[m].start()
+
+        def start(t, carry, m=m):
+            load(m, t).start()
+            return carry
+        lax.fori_loop(0, tiles, start, 0)
+    for m in range(mats):
+        q_copies[m].wait()
+        right = right_ref[m]
+
+        def body(t, carry, m=m, right=right):
+            load(m, t).wait()
+            span = pl.ds(pl.multiple_of(t * tile, tile), tile)
+            approx = lax.dot_general(q_low[m, t], right, (((0,), (0,)), ((), ())),
+                                     preferred_element_type=F32)
+            out[m, span] = (comp[m, span].astype(F32) - approx).astype(BF16)
+            store(m, t).start()
+
+            @pl.when(t == dp)
+            def _():
+                update[m] = approx.astype(BF16)
+            return carry
+        lax.fori_loop(0, tiles, body, 0)
+    update_copy = pltpu.make_async_copy(update, update_hbm, update_sem)
+    update_copy.start()
+    for m in range(mats):
+        def finish(t, carry, m=m):
+            store(m, t).wait()
+            return carry
+        lax.fori_loop(0, tiles, finish, 0)
+    update_copy.wait()
 
 
 def shards(n_dp, n_mp, gradients, feedback, right_factor):
@@ -354,25 +389,24 @@
             dma((mats, n_dp)), dma((mats, n_dp)),
         ],
         compiler_params=pltpu.CompilerParams(
-            collective_id=0, has_side_effects=True, vmem_limit_bytes=48 * 1024 * 1024),
+            collective_id=0, has_side_effects=True, vmem_limit_bytes=40 * 1024 * 1024),
         name="reduce_factors",
-    )(gradients, feedback, right_factor)
+    )(gradients, feedback, jnp.swapaxes(right_factor, 1, 2))
     return pl.pallas_call(
         residue_kernel,
-        grid=(mats, tiles),
         out_shape=(
             jax.ShapeDtypeStruct((1, mats, rows, cols), BF16),
             jax.ShapeDtypeStruct((mats, tile, cols), BF16),
         ),
-        in_specs=[
-            pl.BlockSpec((1, tile, cols), lambda m, t: (m, t, 0)),
-            pl.BlockSpec((1, 1, rank, tile), lambda m, t: (m, t, 0, 0)),
-            pl.BlockSpec((1, rank, cols), lambda m, t: (m, 0, 0)),
+        in_specs=[any_spec, any_spec, vmem_spec],
+        out_specs=(any_spec, any_spec),
+        scratch_shapes=[
+            pltpu.VMEM((mats, rows, cols), BF16),
+            pltpu.VMEM((mats, tiles, rank, tile), BF16),
+            pltpu.VMEM((mats, rows, cols), BF16),
+            pltpu.VMEM((mats, tile, cols), BF16),
+            dma((mats, tiles)), dma((mats,)), dma((mats, tiles)), dma,
         ],
-        out_specs=(
-            pl.BlockSpec((1, 1, tile, cols), lambda m, t: (0, m, t, 0)),
-            pl.BlockSpec((1, tile, cols), lambda m, t: (m, 0, 0)),
-        ),
         compiler_params=pltpu.CompilerParams(vmem_limit_bytes=24 * 1024 * 1024),
         name="subtract_approx",
     )(comp, q_low, right_low)

time: 57 us -> 50.4 us (0.88)
  local copies, waits for them, and re-layouts: 4.25 us -> 0.75 us
  Pallas kernels: 51.8 us -> 48.8 us
    unnamed x3 -> x2, local copies, waits for them, and re-layouts: 4.25 us -> 0.75 us
    pallas_call x1, Pallas kernels: 9.75 us -> 7.66 us  [shards(): pl.pallas_call(residue_kernel, out_shape=(jax.ShapeDtypeStruct((1, mats,...]
    pallas_call x1, Pallas kernels: 42.1 us -> 41.1 us  [shards(): pl.pallas_call(functools.partial(reduce_kernel, n_dp, n_mp), out_shape=(j...]
where the time goes in v2:
time: 50.4 us; the launch traced here: 50.2 us
  Pallas kernels  48.8 us (97%)
  local copies, waits for them, and re-layouts  0.75 us (1%)
  between operations  0.65 us (1%)
    pallas_call x1, Pallas kernels, shards(): pl.pallas_call(functools.partial(reduce_kernel, n_dp, n_mp), out_shape=(j...  41.1 us
    pallas_call x1, Pallas kernels, shards(): pl.pallas_call(residue_kernel, out_shape=(jax.ShapeDtypeStruct((1, mats,...  7.66 us

profile of v2, /device:TPU:0, one launch (start us, length us, event | category | flops | bytes accessed | tf_op | source)
XLA Modules:
  0.0 50.2 jit_solution(17824985243359629574)
XLA Ops:
  0.6 0.0 copy-start
  0.6 0.7 %copy-done = f32[2,256,16]{1,2,0:T(8,128)S(1)} copy-done((f32[2,256,16]{1,2,0:T(8,128)S(1)}, f32[2,256,16]{1,2,0:T(8,128)}, u32[]{:S(2)}) %copy-start) | copy-done | bytes 32792
  1.4 41.1 %reduce_factors.1 = (bf16[2,8192,256]{2,1,0:T(8,128)(2,1)S(1)}, bf16[2,8,16,1024]{3,2,1,0:T(8,128)(2,1)S(1)}, bf16[2,16,256]{2,1,0:T(8,128)(2,1)S(1)}) custom-call(bf16[1,2,8192,256]{3,2,1,0:T(8,128)(2,1)} %grad_hbm.1, bf16[1,2,8192,256]{3,2,1,0:T(8,128)(2,1)} %feed_hbm.1, f32[2,16,256]{2,1,0:T(8,128)S(1)} %bitcast.1), custom_call_target="tpu_custom_call" | custom-call | tf_op jit(solution)/shard_map/reduce_factors/pallas_call | solution.py:360
  42.5 7.7 %subtract_approx.1 = (bf16[1,2,8192,256]{3,2,1,0:T(8,128)(2,1)}, bf16[2,1024,256]{2,1,0:T(8,128)(2,1)}) custom-call(bf16[2,8192,256]{2,1,0:T(8,128)(2,1)S(1)} %get-tuple-element.5.comp_hbm, bf16[2,8,16,1024]{3,2,1,0:T(8,128)(2,1)S(1)} %get-tuple-element.6.q_hbm, bf16[2,16,256]{2,1,0:T(8,128)(2,1)S(1)} %get-tuple-element.7.right_ref), custom_call_target="tpu_custom_call" | custom-call | tf_op jit(solution)/shard_map/subtract_approx/pallas_call | solution.py:395
Async XLA Ops:
  0.6 0.8 %copy-start = (f32[2,256,16]{1,2,0:T(8,128)S(1)}, f32[2,256,16]{1,2,0:T(8,128)}, u32[]{:S(2)}) copy-start(f32[2,256,16]{1,2,0:T(8,128)} %param.5) | copy-start | bytes 98308

commit v3 on v2

--- a/solution.py
+++ b/solution.py
@@ -29,16 +29,20 @@
     return lax.dot_general(left, right, (((1,), (0,)), ((), ())), preferred_element_type=F32)
 
 
+def tn_dot(left, right):
+    return lax.dot_general(left, right, (((0,), (0,)), ((), ())), preferred_element_type=F32)
+
+
 def reduce_kernel(
     n_dp, n_mp,
     grad_hbm, feed_hbm, right_ref,
     comp_hbm, q_hbm, right_low_ref,
-    comp, feed, part, half, from_core, from_chip, plane, from_z, full,
-    gram_chip, gram_core, q_low, right_all,
+    comp, feed, part, half, half_low, from_core, from_chip, plane, plane_low, from_z, full,
+    gram_all, q_low, right_all,
     load_sem, store_sem, qstore_sem,
     core_send, core_recv, chip_send, chip_recv, z_send, z_recv,
     zg_send, zg_recv, cg_send, cg_recv, kg_send, kg_recv,
-    gc_send, gc_recv, gk_send, gk_recv, r_send, r_recv,
+    gram_send, gram_recv, r_send, r_recv,
 ):
     mats, rows, cols = comp.shape
     rank = right_ref.shape[1]
@@ -119,12 +123,14 @@
 
     def core_finish(m):
         landed(from_core.at[m], core_send.at[m], core_recv.at[m])
-        half[m] = part[m, pl.ds(core * half_blocks, half_blocks)] + from_core[m]
+        total = part[m, pl.ds(core * half_blocks, half_blocks)] + from_core[m]
+        half[m] = total
+        half_low[m] = total.astype(BF16)
 
     def chip_start(m):
         for k in range(1, chips):
             to = lax.rem(chip + k, chips)
-            send(half.at[m, pl.ds(to * chip_blocks, chip_blocks)], from_chip.at[m, chip],
+            send(half_low.at[m, pl.ds(to * chip_blocks, chip_blocks)], from_chip.at[m, chip],
                  chip_send.at[m, k], chip_recv.at[m, chip], (to * CORES + core, z))
 
     def chip_finish(m):
@@ -132,14 +138,15 @@
         for k in range(1, chips):
             source = lax.rem(chip + k, chips)
             landed(from_chip.at[m, source], chip_send.at[m, k], chip_recv.at[m, source])
-            total = total + from_chip[m, source]
+            total = total + from_chip[m, source].astype(F32)
         plane[m] = total
+        plane_low[m] = total.astype(BF16)
 
     def z_start(m):
         for k in range(1, n_mp):
             to = lax.rem(z + k, n_mp)
             first = to * z_blocks if z_split else 0
-            send(plane.at[m, pl.ds(first, z_blocks)], from_z.at[m, z],
+            send(plane_low.at[m, pl.ds(first, z_blocks)], from_z.at[m, z],
                  z_send.at[m, k], z_recv.at[m, z], (dp, to))
 
     base = core * half_blocks + chip * chip_blocks
@@ -150,7 +157,7 @@
         for k in range(1, n_mp):
             source = lax.rem(z + k, n_mp)
             landed(from_z.at[m, source], z_send.at[m, k], z_recv.at[m, source])
-            total = total + from_z[m, source]
+            total = total + from_z[m, source].astype(F32)
         full[m, mine] = total * (1.0 / n_dp)
 
     def z_gather_start(m):
@@ -169,51 +176,46 @@
     gram_lane = 6 * rank
 
     def chip_gather_start(m):
-        own = pl.ds(base, chip_blocks)
-        for k in range(1, chips):
-            to = lax.rem(chip + k, chips)
-            send(full.at[m, own], full.at[m, own], cg_send.at[m, k], cg_recv.at[m, chip],
-                 (to * CORES + core, z))
         value = jnp.concatenate([full[m, base + j] for j in range(chip_blocks)], axis=1)
         terms = split3(value)
         tall = jnp.concatenate(terms, axis=0)
         pad = jnp.zeros((gram_lane, value.shape[1]), BF16)
         wide = sum(nt_dot(tall, jnp.concatenate([pad, term], axis=0)) for term in terms)
         gram = wide[0:rank] + wide[rank:2 * rank] + wide[2 * rank:3 * rank]
-        gram_chip[m, chip] = jnp.zeros((rank, LANES), F32)
-        gram_chip[m, chip, :, 0:gram_lane + rank] = gram
+        gram_all[m, dp] = jnp.zeros((rank, LANES), F32)
+        gram_all[m, dp, :, 0:gram_lane + rank] = gram
+        for k in range(1, n_dp):
+            send(gram_all.at[m, dp], gram_all.at[m, dp], gram_send.at[m, k], gram_recv.at[m, dp],
+                 (lax.rem(dp + k, n_dp), z))
+        own = pl.ds(base, chip_blocks)
         for k in range(1, chips):
             to = lax.rem(chip + k, chips)
-            send(gram_chip.at[m, chip], gram_chip.at[m, chip], gc_send.at[m, k],
-                 gc_recv.at[m, chip], (to * CORES + core, z))
+            send(full.at[m, own], full.at[m, own], cg_send.at[m, k], cg_recv.at[m, chip],
+                 (to * CORES + core, z))
 
     def chip_gather_finish(m):
         for k in range(1, chips):
             source = lax.rem(chip + k, chips)
             landed(full.at[m, pl.ds(core * half_blocks + source * chip_blocks, chip_blocks)],
                    cg_send.at[m, k], cg_recv.at[m, source])
-            landed(gram_chip.at[m, source], gc_send.at[m, k], gc_recv.at[m, source])
 
     def core_gather_start(m):
         own = pl.ds(core * half_blocks, half_blocks)
         send(full.at[m, own], full.at[m, own], kg_send.at[m], kg_recv.at[m], (twin, z))
-        total = gram_chip[m, 0]
-        for c in range(1, chips):
-            total = total + gram_chip[m, c]
-        gram_core[m, core] = total
-        send(gram_core.at[m, core], gram_core.at[m, core], gk_send.at[m], gk_recv.at[m], (twin, z))
 
     def core_gather_finish(m):
-        landed(gram_core.at[m, other], gk_send.at[m], gk_recv.at[m])
         landed(full.at[m, pl.ds(other * half_blocks, half_blocks)], kg_send.at[m], kg_recv.at[m])
 
     row_at = lax.broadcasted_iota(jnp.int32, (rank, LANES), 0)
     lane_at = lax.broadcasted_iota(jnp.int32, (rank, LANES), 1)
 
     def inverse_factor(m):
-        gram = gram_core[m, 0]
-        for c in range(1, CORES):
-            gram = gram + gram_core[m, c]
+        for k in range(1, n_dp):
+            source = lax.rem(dp + k, n_dp)
+            landed(gram_all.at[m, source], gram_send.at[m, k], gram_recv.at[m, source])
+        gram = gram_all[m, 0]
+        for c in range(1, n_dp):
+            gram = gram + gram_all[m, c]
         copies = (lane_at < gram_lane) & (lax.rem(lane_at, rank) == row_at)
         work = jnp.where(copies, 1.0, gram)
         for k in range(rank):
@@ -225,8 +227,7 @@
         diagonal = jnp.sum(jnp.where(lane_at == row_at + gram_lane, work, 0.0), axis=1, keepdims=True)
         return work / jnp.sqrt(diagonal)
 
-    def project(m):
-        inverse = inverse_factor(m)
+    def project(m, inverse):
         high, middle, low = split3(inverse)
         group = lane_at // rank
         left = jnp.where((group == 2) | (group == 3), middle.astype(F32),
@@ -241,7 +242,7 @@
             span = pl.ds(pl.multiple_of(t * tile, tile), tile)
             return total + nn_dot(q, comp[m, span])
         total = lax.fori_loop(0, tiles, body, jnp.zeros((rank, cols), F32), unroll=4)
-        right_all[m, dp] = total
+        right_all[m, dp] = total.astype(BF16)
         for k in range(1, n_dp):
             send(right_all.at[m, dp], right_all.at[m, dp], r_send.at[m, k], r_recv.at[m, dp],
                  (lax.rem(dp + k, n_dp), z))
@@ -251,9 +252,9 @@
         for k in range(1, n_dp):
             source = lax.rem(dp + k, n_dp)
             landed(right_all.at[m, source], r_send.at[m, k], r_recv.at[m, source])
-        total = right_all[m, 0]
+        total = right_all[m, 0].astype(F32)
         for c in range(1, n_dp):
-            total = total + right_all[m, c]
+            total = total + right_all[m, c].astype(F32)
         right_low_ref[m] = (total * (1.0 / n_dp)).astype(BF16)
 
     pairs = [(core_finish, chip_start), (chip_finish, z_start), (z_finish, z_gather_start),
@@ -275,13 +276,15 @@
     advance(1, 1)
     advance(0, 3)
     advance(1, 2)
+    inverse_0 = inverse_factor(0)
     advance(0, 4)
     advance(1, 3)
     core_gather_finish(0)
-    project(0)
+    project(0, inverse_0)
     advance(1, 4)
+    inverse_1 = inverse_factor(1)
     core_gather_finish(1)
-    project(1)
+    project(1, inverse_1)
     right_finish(0)
     right_finish(1)
     for copy in sent:
@@ -299,6 +302,7 @@
 def residue_kernel(comp_hbm, q_hbm, right_ref, feed_hbm, update_hbm, comp, q_low, out, update,
                    load_sem, q_sem, store_sem, update_sem):
     mats, tiles, _, tile = q_low.shape
+    piece = min(tile, 2 * LANES)
     dp = lax.axis_index("dp")
 
     def load(m, t):
@@ -323,17 +327,16 @@
 
         def body(t, carry, m=m, right=right):
             load(m, t).wait()
-            span = pl.ds(pl.multiple_of(t * tile, tile), tile)
-            approx = lax.dot_general(q_low[m, t], right, (((0,), (0,)), ((), ())),
-                                     preferred_element_type=F32)
-            out[m, span] = (comp[m, span].astype(F32) - approx).astype(BF16)
+            for r in range(0, tile, piece):
+                approx = tn_dot(q_low[m, t, :, r:r + piece], right)
+                rows = pl.ds(pl.multiple_of(t * tile + r, piece), piece)
+                out[m, rows] = (comp[m, rows].astype(F32) - approx).astype(BF16)
             store(m, t).start()
-
-            @pl.when(t == dp)
-            def _():
-                update[m] = approx.astype(BF16)
             return carry
         lax.fori_loop(0, tiles, body, 0)
+    for m in range(mats):
+        for r in range(0, tile, piece):
+            update[m, r:r + piece] = tn_dot(q_low[m, dp, :, r:r + piece], right_ref[m]).astype(BF16)
     update_copy = pltpu.make_async_copy(update, update_hbm, update_sem)
     update_copy.start()
     for m in range(mats):
@@ -371,22 +374,22 @@
             pltpu.VMEM((mats, rows, cols), BF16),
             pltpu.VMEM((mats, blocks, rank, LANES), F32),
             pltpu.VMEM((mats, half_blocks, rank, LANES), F32),
+            pltpu.VMEM((mats, half_blocks, rank, LANES), BF16),
             pltpu.VMEM((mats, half_blocks, rank, LANES), F32),
-            pltpu.VMEM((mats, chips, chip_blocks, rank, LANES), F32),
+            pltpu.VMEM((mats, chips, chip_blocks, rank, LANES), BF16),
             pltpu.VMEM((mats, chip_blocks, rank, LANES), F32),
-            pltpu.VMEM((mats, n_mp, z_blocks, rank, LANES), F32),
+            pltpu.VMEM((mats, chip_blocks, rank, LANES), BF16),
+            pltpu.VMEM((mats, n_mp, z_blocks, rank, LANES), BF16),
             pltpu.VMEM((mats, blocks, rank, LANES), F32),
-            pltpu.VMEM((mats, chips, rank, LANES), F32),
-            pltpu.VMEM((mats, CORES, rank, LANES), F32),
+            pltpu.VMEM((mats, n_dp, rank, LANES), F32),
             pltpu.VMEM((mats, tiles, rank, tile), BF16),
-            pltpu.VMEM((mats, n_dp, rank, cols), F32),
+            pltpu.VMEM((mats, n_dp, rank, cols), BF16),
             dma((2, mats, tiles)), dma((mats, tiles)), dma((mats,)),
             dma((mats,)), dma((mats,)), dma((mats, chips)), dma((mats, chips)),
             dma((mats, n_mp)), dma((mats, n_mp)),
             dma((mats, n_mp)), dma((mats, n_mp)), dma((mats, chips)), dma((mats, chips)),
             dma((mats,)), dma((mats,)),
-            dma((mats, chips)), dma((mats, chips)), dma((mats,)), dma((mats,)),
-            dma((mats, n_dp)), dma((mats, n_dp)),
+            dma((mats, n_dp)), dma((mats, n_dp)), dma((mats, n_dp)), dma((mats, n_dp)),
         ],
         compiler_params=pltpu.CompilerParams(
             collective_id=0, has_side_effects=True, vmem_limit_bytes=40 * 1024 * 1024),

time: 50.4 us -> 49.8 us (0.988)
  Pallas kernels: 48.8 us -> 48.2 us
    pallas_call x1, Pallas kernels: 41.1 us -> 40.4 us  [shards(): pl.pallas_call(functools.partial(reduce_kernel, n_dp, n_mp), out_shape=(j...]
where the time goes in v3:
time: 49.8 us; the launch traced here: 49.6 us
  Pallas kernels  48.2 us (97%)
  local copies, waits for them, and re-layouts  0.75 us (2%)
  between operations  0.65 us (1%)
    pallas_call x1, Pallas kernels, shards(): pl.pallas_call(functools.partial(reduce_kernel, n_dp, n_mp), out_shape=(j...  40.4 us
    pallas_call x1, Pallas kernels, shards(): pl.pallas_call(residue_kernel, out_shape=(jax.ShapeDtypeStruct((1, mats,...  7.83 us

profile of v3, /device:TPU:0, one launch (start us, length us, event | category | flops | bytes accessed | tf_op | source)
XLA Modules:
  0.0 49.6 jit_solution(18422145075341224271)
XLA Ops:
  0.6 0.0 copy-start
  0.6 0.7 %copy-done = f32[2,256,16]{1,2,0:T(8,128)S(1)} copy-done((f32[2,256,16]{1,2,0:T(8,128)S(1)}, f32[2,256,16]{1,2,0:T(8,128)}, u32[]{:S(2)}) %copy-start) | copy-done | bytes 32792
  1.4 40.4 %reduce_factors.1 = (bf16[2,8192,256]{2,1,0:T(8,128)(2,1)S(1)}, bf16[2,8,16,1024]{3,2,1,0:T(8,128)(2,1)S(1)}, bf16[2,16,256]{2,1,0:T(8,128)(2,1)S(1)}) custom-call(bf16[1,2,8192,256]{3,2,1,0:T(8,128)(2,1)} %grad_hbm.1, bf16[1,2,8192,256]{3,2,1,0:T(8,128)(2,1)} %feed_hbm.1, f32[2,16,256]{2,1,0:T(8,128)S(1)} %bitcast.1), custom_call_target="tpu_custom_call" | custom-call | tf_op jit(solution)/shard_map/reduce_factors/pallas_call | solution.py:363
  41.8 7.8 %subtract_approx.1 = (bf16[1,2,8192,256]{3,2,1,0:T(8,128)(2,1)}, bf16[2,1024,256]{2,1,0:T(8,128)(2,1)}) custom-call(bf16[2,8192,256]{2,1,0:T(8,128)(2,1)S(1)} %get-tuple-element.5.comp_hbm, bf16[2,8,16,1024]{3,2,1,0:T(8,128)(2,1)S(1)} %get-tuple-element.6.q_hbm, bf16[2,16,256]{2,1,0:T(8,128)(2,1)S(1)} %get-tuple-element.7.right_ref), custom_call_target="tpu_custom_call" | custom-call | tf_op jit(solution)/shard_map/subtract_approx/pallas_call | solution.py:398
Async XLA Ops:
  0.6 0.8 %copy-start = (f32[2,256,16]{1,2,0:T(8,128)S(1)}, f32[2,256,16]{1,2,0:T(8,128)}, u32[]{:S(2)}) copy-start(f32[2,256,16]{1,2,0:T(8,128)} %param.5) | copy-start | bytes 98308

commit v4 on v3

--- a/solution.py
+++ b/solution.py
@@ -36,10 +36,10 @@
 def reduce_kernel(
     n_dp, n_mp,
     grad_hbm, feed_hbm, right_ref,
-    comp_hbm, q_hbm, right_low_ref,
-    comp, feed, part, half, half_low, from_core, from_chip, plane, plane_low, from_z, full,
-    gram_all, q_low, right_all,
-    load_sem, store_sem, qstore_sem,
+    comp, q_low, right_low_ref,
+    feed, part, half, half_low, from_core, from_chip, plane, plane_low, from_z, full,
+    gram_all, right_all,
+    load_sem,
     core_send, core_recv, chip_send, chip_recv, z_send, z_recv,
     zg_send, zg_recv, cg_send, cg_recv, kg_send, kg_recv,
     gram_send, gram_recv, r_send, r_recv,
@@ -113,7 +113,6 @@
             term = nt_dot(right_t, value)
             for j in range(per_tile):
                 part[m, t * per_tile + j] = term[:, j * LANES:(j + 1) * LANES]
-            pltpu.make_async_copy(comp.at[m, span], comp_hbm.at[m, span], store_sem.at[m, t]).start()
             return carry
         lax.fori_loop(first, last, body, 0)
 
@@ -246,7 +245,6 @@
         for k in range(1, n_dp):
             send(right_all.at[m, dp], right_all.at[m, dp], r_send.at[m, k], r_recv.at[m, dp],
                  (lax.rem(dp + k, n_dp), z))
-        pltpu.make_async_copy(q_low.at[m], q_hbm.at[m], qstore_sem.at[m]).start()
 
     def right_finish(m):
         for k in range(1, n_dp):
@@ -289,44 +287,21 @@
     right_finish(1)
     for copy in sent:
         copy.wait_send()
-    for m in range(mats):
-        pltpu.make_async_copy(q_low.at[m], q_hbm.at[m], qstore_sem.at[m]).wait()
-
-        def end_store(t, carry, m=m):
-            span = pl.ds(t * tile, tile)
-            pltpu.make_async_copy(comp.at[m, span], comp_hbm.at[m, span], store_sem.at[m, t]).wait()
-            return carry
-        lax.fori_loop(0, tiles, end_store, 0)
-
-
-def residue_kernel(comp_hbm, q_hbm, right_ref, feed_hbm, update_hbm, comp, q_low, out, update,
-                   load_sem, q_sem, store_sem, update_sem):
+
+
+def residue_kernel(comp, q_low, right_ref, feed_hbm, update_hbm, out, update, store_sem, update_sem):
     mats, tiles, _, tile = q_low.shape
     piece = min(tile, 2 * LANES)
     dp = lax.axis_index("dp")
 
-    def load(m, t):
-        span = pl.ds(t * tile, tile)
-        return pltpu.make_async_copy(comp_hbm.at[m, span], comp.at[m, span], load_sem.at[m, t])
-
     def store(m, t):
         span = pl.ds(t * tile, tile)
         return pltpu.make_async_copy(out.at[m, span], feed_hbm.at[0, m, span], store_sem.at[m, t])
 
-    q_copies = [pltpu.make_async_copy(q_hbm.at[m], q_low.at[m], q_sem.at[m]) for m in range(mats)]
     for m in range(mats):
-        q_copies[m].start()
-
-        def start(t, carry, m=m):
-            load(m, t).start()
-            return carry
-        lax.fori_loop(0, tiles, start, 0)
-    for m in range(mats):
-        q_copies[m].wait()
         right = right_ref[m]
 
         def body(t, carry, m=m, right=right):
-            load(m, t).wait()
             for r in range(0, tile, piece):
                 approx = tn_dot(q_low[m, t, :, r:r + piece], right)
                 rows = pl.ds(pl.multiple_of(t * tile + r, piece), piece)
@@ -368,9 +343,8 @@
             jax.ShapeDtypeStruct((mats, rank, cols), BF16),
         ),
         in_specs=[any_spec, any_spec, vmem_spec],
-        out_specs=(any_spec, any_spec, vmem_spec),
+        out_specs=(vmem_spec, vmem_spec, vmem_spec),
         scratch_shapes=[
-            pltpu.VMEM((mats, rows, cols), BF16),
             pltpu.VMEM((mats, rows, cols), BF16),
             pltpu.VMEM((mats, blocks, rank, LANES), F32),
             pltpu.VMEM((mats, half_blocks, rank, LANES), F32),
@@ -382,9 +356,8 @@
             pltpu.VMEM((mats, n_mp, z_blocks, rank, LANES), BF16),
             pltpu.VMEM((mats, blocks, rank, LANES), F32),
             pltpu.VMEM((mats, n_dp, rank, LANES), F32),
-            pltpu.VMEM((mats, tiles, rank, tile), BF16),
             pltpu.VMEM((mats, n_dp, rank, cols), BF16),
-            dma((2, mats, tiles)), dma((mats, tiles)), dma((mats,)),
+            dma((2, mats, tiles)),
             dma((mats,)), dma((mats,)), dma((mats, chips)), dma((mats, chips)),
             dma((mats, n_mp)), dma((mats, n_mp)),
             dma((mats, n_mp)), dma((mats, n_mp)), dma((mats, chips)), dma((mats, chips)),
@@ -392,7 +365,7 @@
             dma((mats, n_dp)), dma((mats, n_dp)), dma((mats, n_dp)), dma((mats, n_dp)),
         ],
         compiler_params=pltpu.CompilerParams(
-            collective_id=0, has_side_effects=True, vmem_limit_bytes=40 * 1024 * 1024),
+            collective_id=0, has_side_effects=True, vmem_limit_bytes=44 * 1024 * 1024),
         name="reduce_factors",
     )(gradients, feedback, jnp.swapaxes(right_factor, 1, 2))
     return pl.pallas_call(
@@ -401,14 +374,12 @@
             jax.ShapeDtypeStruct((1, mats, rows, cols), BF16),
             jax.ShapeDtypeStruct((mats, tile, cols), BF16),
         ),
-        in_specs=[any_spec, any_spec, vmem_spec],
+        in_specs=[vmem_spec, vmem_spec, vmem_spec],
         out_specs=(any_spec, any_spec),
         scratch_shapes=[
             pltpu.VMEM((mats, rows, cols), BF16),
-            pltpu.VMEM((mats, tiles, rank, tile), BF16),
-            pltpu.VMEM((mats, rows, cols), BF16),
             pltpu.VMEM((mats, tile, cols), BF16),
-            dma((mats, tiles)), dma((mats,)), dma((mats, tiles)), dma,
+            dma((mats, tiles)), dma,
         ],
         compiler_params=pltpu.CompilerParams(vmem_limit_bytes=24 * 1024 * 1024),
         name="subtract_approx",

time: 49.8 us -> 48.2 us (0.968)
  Pallas kernels: 48.2 us -> 46.7 us
    pallas_call x1, Pallas kernels: 7.83 us -> 6.93 us  [shards(): pl.pallas_call(residue_kernel, out_shape=(jax.ShapeDtypeStruct((1, mats,...]
    pallas_call x1, Pallas kernels: 40.4 us -> 39.7 us  [shards(): pl.pallas_call(functools.partial(reduce_kernel, n_dp, n_mp), out_shape=(j...]
where the time goes in v4:
time: 48.2 us; the launch traced here: 48 us
  Pallas kernels  46.7 us (97%)
  local copies, waits for them, and re-layouts  0.75 us (2%)
  between operations  0.65 us (1%)
    pallas_call x1, Pallas kernels, shards(): pl.pallas_call(functools.partial(reduce_kernel, n_dp, n_mp), out_shape=(j...  39.7 us
    pallas_call x1, Pallas kernels, shards(): pl.pallas_call(residue_kernel, out_shape=(jax.ShapeDtypeStruct((1, mats,...  6.93 us

profile of v4, /device:TPU:0, one launch (start us, length us, event | category | flops | bytes accessed | tf_op | source)
XLA Modules:
  0.0 48.0 jit_solution(13189793966920430380)
XLA Ops:
  0.6 0.0 copy-start
  0.6 0.7 %copy-done = f32[2,256,16]{1,2,0:T(8,128)S(1)} copy-done((f32[2,256,16]{1,2,0:T(8,128)S(1)}, f32[2,256,16]{1,2,0:T(8,128)}, u32[]{:S(2)}) %copy-start) | copy-done | bytes 32792
  1.4 39.7 %reduce_factors.1 = (bf16[2,8192,256]{2,1,0:T(8,128)(2,1)S(1)}, bf16[2,8,16,1024]{3,2,1,0:T(8,128)(2,1)S(1)}, bf16[2,16,256]{2,1,0:T(8,128)(2,1)S(1)}) custom-call(bf16[1,2,8192,256]{3,2,1,0:T(8,128)(2,1)} %grad_hbm.1, bf16[1,2,8192,256]{3,2,1,0:T(8,128)(2,1)} %feed_hbm.1, f32[2,16,256]{2,1,0:T(8,128)S(1)} %bitcast.1), custom_call_target="tpu_custom_call" | custom-call | tf_op jit(solution)/shard_map/reduce_factors/pallas_call | solution.py:338
  41.1 6.9 %subtract_approx.1 = (bf16[1,2,8192,256]{3,2,1,0:T(8,128)(2,1)}, bf16[2,1024,256]{2,1,0:T(8,128)(2,1)}) custom-call(bf16[2,8192,256]{2,1,0:T(8,128)(2,1)S(1)} %get-tuple-element.5.comp, bf16[2,8,16,1024]{3,2,1,0:T(8,128)(2,1)S(1)} %get-tuple-element.6.q_low, bf16[2,16,256]{2,1,0:T(8,128)(2,1)S(1)} %get-tuple-element.7.right_ref), custom_call_target="tpu_custom_call" | custom-call | tf_op jit(solution)/shard_map/subtract_approx/pallas_call | solution.py:371
Async XLA Ops:
  0.6 0.8 %copy-start = (f32[2,256,16]{1,2,0:T(8,128)S(1)}, f32[2,256,16]{1,2,0:T(8,128)}, u32[]{:S(2)}) copy-start(f32[2,256,16]{1,2,0:T(8,128)} %param.5) | copy-start | bytes 98308

commit v5 on v4

--- a/solution.py
+++ b/solution.py
@@ -308,7 +308,7 @@
                 out[m, rows] = (comp[m, rows].astype(F32) - approx).astype(BF16)
             store(m, t).start()
             return carry
-        lax.fori_loop(0, tiles, body, 0)
+        lax.fori_loop(0, tiles, body, 0, unroll=4)
     for m in range(mats):
         for r in range(0, tile, piece):
             update[m, r:r + piece] = tn_dot(q_low[m, dp, :, r:r + piece], right_ref[m]).astype(BF16)

time: 48.2 us -> 45.9 us (0.952)
  Pallas kernels: 46.7 us -> 44.3 us
    pallas_call x1, Pallas kernels: 6.93 us -> 4.62 us  [shards(): pl.pallas_call(residue_kernel, out_shape=(jax.ShapeDtypeStruct((1, mats,...]
where the time goes in v5:
time: 45.9 us; the launch traced here: 45.7 us
  Pallas kernels  44.3 us (97%)
  local copies, waits for them, and re-layouts  0.75 us (2%)
  between operations  0.65 us (1%)
    pallas_call x1, Pallas kernels, shards(): pl.pallas_call(functools.partial(reduce_kernel, n_dp, n_mp), out_shape=(j...  39.7 us
    pallas_call x1, Pallas kernels, shards(): pl.pallas_call(residue_kernel, out_shape=(jax.ShapeDtypeStruct((1, mats,...  4.62 us

profile of v5, /device:TPU:0, one launch (start us, length us, event | category | flops | bytes accessed | tf_op | source)
XLA Modules:
  0.0 45.7 jit_solution(17422048335004346645)
XLA Ops:
  0.6 0.0 copy-start
  0.6 0.7 %copy-done = f32[2,256,16]{1,2,0:T(8,128)S(1)} copy-done((f32[2,256,16]{1,2,0:T(8,128)S(1)}, f32[2,256,16]{1,2,0:T(8,128)}, u32[]{:S(2)}) %copy-start) | copy-done | bytes 32792
  1.4 39.7 %reduce_factors.1 = (bf16[2,8192,256]{2,1,0:T(8,128)(2,1)S(1)}, bf16[2,8,16,1024]{3,2,1,0:T(8,128)(2,1)S(1)}, bf16[2,16,256]{2,1,0:T(8,128)(2,1)S(1)}) custom-call(bf16[1,2,8192,256]{3,2,1,0:T(8,128)(2,1)} %grad_hbm.1, bf16[1,2,8192,256]{3,2,1,0:T(8,128)(2,1)} %feed_hbm.1, f32[2,16,256]{2,1,0:T(8,128)S(1)} %bitcast.1), custom_call_target="tpu_custom_call" | custom-call | tf_op jit(solution)/shard_map/reduce_factors/pallas_call | solution.py:338
  41.1 4.6 %subtract_approx.1 = (bf16[1,2,8192,256]{3,2,1,0:T(8,128)(2,1)}, bf16[2,1024,256]{2,1,0:T(8,128)(2,1)}) custom-call(bf16[2,8192,256]{2,1,0:T(8,128)(2,1)S(1)} %get-tuple-element.5.comp, bf16[2,8,16,1024]{3,2,1,0:T(8,128)(2,1)S(1)} %get-tuple-element.6.q_low, bf16[2,16,256]{2,1,0:T(8,128)(2,1)S(1)} %get-tuple-element.7.right_ref), custom_call_target="tpu_custom_call" | custom-call | tf_op jit(solution)/shard_map/subtract_approx/pallas_call | solution.py:371
Async XLA Ops:
  0.6 0.8 %copy-start = (f32[2,256,16]{1,2,0:T(8,128)S(1)}, f32[2,256,16]{1,2,0:T(8,128)}, u32[]{:S(2)}) copy-start(f32[2,256,16]{1,2,0:T(8,128)} %param.5) | copy-start | bytes 98308
